TPU v7x, 32 devices: a whole 2x2x4 slice. The times are simulated.
32 devices in a mesh: tm: 8 (over z, core), head: 4 (over y, x).
Axes of the slice: x: 2, y: 2, z: 4, core: 2. Of those that a mesh axis runs over, the one named last changes fastest.
Arguments:
- queries: bfloat16 [8192, 2048], P(('tm', 'head')), may hold values from -200 to 200
- key_rows: bfloat16 [8192, 2048], P(('tm', 'head')), may hold values from -6 to 6
- value_rows: bfloat16 [8192, 2048], P(('tm', 'head')), may hold values from -6 to 6
- grad_out: bfloat16 [8192, 2048], P(('tm', 'head')), may hold values from -6 to 6
- tile_lists: int32 [64, 17], replicated, may hold values from -1 to 63, as said below
Outputs:
- attended: bfloat16 [8192, 2048], P(('tm', 'head'))
- grad_queries: bfloat16 [8192, 2048], P(('tm', 'head'))
- grad_keys: bfloat16 [8192, 2048], P(('tm', 'head'))
- grad_values: bfloat16 [8192, 2048], P(('tm', 'head'))
Inputs may be any that keep to these rules, and one draw needn't show every extreme that they name: Row i of tile_lists holds i + o for each of 17 offsets o, in the same order in every row; the offsets are distinct, 0, 1, -1, 32 and -(32) among them, and o is one of them exactly when -o is; the entry is -1 where i + o lies outside 0 to 63.
All inputs are finite; a program needn't handle non-finite values.
Results may differ from a plain program's by a relative error of at most 0.03.
Values may be sent and summed in bfloat16 or wider, within the bound.
A program may use at most 384 MiB of HBM per device.

v0:
```python
import math

import jax
import jax.numpy as jnp
from jax import lax
from jax.sharding import PartitionSpec as P

HEAD_DIM = 128
HEADS = 16
BLOCK = 128


def slab_stack(doubled, start_tile, offsets, group, tile_total, slot_count):
    pieces = []
    for slot in range(slot_count):
        where_at = jnp.mod(start_tile + offsets[slot], tile_total)
        pieces.append(lax.dynamic_slice_in_dim(doubled, where_at, group, 0))
    return jnp.stack(pieces, 0)


def add_slabs(accum, parts, start_tile, offsets, group, tile_total, slot_count):
    for slot in range(slot_count):
        where_at = jnp.mod(start_tile + offsets[slot], tile_total)
        current = lax.dynamic_slice_in_dim(accum, where_at, group, 0)
        accum = lax.dynamic_update_slice_in_dim(accum, current + parts[slot], where_at, 0)
    return accum


def on_device(queries, key_rows, value_rows, grad_out, tile_lists):
    heads_here = HEADS // lax.axis_size("head")
    arrived = (
        lax.all_to_all(queries, "head", split_axis=1, concat_axis=0, tiled=True),
        lax.all_to_all(key_rows, "head", split_axis=1, concat_axis=0, tiled=True),
        lax.all_to_all(value_rows, "head", split_axis=1, concat_axis=0, tiled=True),
        lax.all_to_all(grad_out, "head", split_axis=1, concat_axis=0, tiled=True),
    )
    tokens_here = arrived[0].shape[0]
    query_loc = arrived[0].reshape(tokens_here, heads_here, HEAD_DIM)
    key_loc = arrived[1].reshape(tokens_here, heads_here, HEAD_DIM)
    value_loc = arrived[2].reshape(tokens_here, heads_here, HEAD_DIM)
    grad_loc = arrived[3].reshape(tokens_here, heads_here, HEAD_DIM)
    scaling = HEAD_DIM ** (-0.5)
    local_tiles = tokens_here // BLOCK
    tile_total = tile_lists.shape[0]
    slot_count = tile_lists.shape[1]
    group = math.gcd(local_tiles, max(1, 512 // BLOCK))
    group_count = local_tiles // group
    first_tile = lax.axis_index("tm") * local_tiles
    row_index = jnp.arange(tile_total, dtype=jnp.int32)[:, None]
    offsets = jnp.max(jnp.where(tile_lists >= 0, tile_lists - row_index, -2 * tile_total), axis=0)
    own_lists = lax.dynamic_slice_in_dim(tile_lists, first_tile, local_tiles, 0)
    live_slot = own_lists >= 0
    whole_keys, whole_values = (
        lax.all_gather(key_loc, "tm", axis=0, tiled=True),
        lax.all_gather(value_loc, "tm", axis=0, tiled=True),
    )
    key_tiles = whole_keys.reshape(tile_total, BLOCK, heads_here, HEAD_DIM)
    value_tiles = whole_values.reshape(tile_total, BLOCK, heads_here, HEAD_DIM)
    doubled_keys = jnp.concatenate([key_tiles, key_tiles], 0)
    doubled_values = jnp.concatenate([value_tiles, value_tiles], 0)
    query_tiles = query_loc.reshape(local_tiles, BLOCK, heads_here, HEAD_DIM)
    grad_tiles = grad_loc.reshape(local_tiles, BLOCK, heads_here, HEAD_DIM)

    def forward_group(group_idx):
        offset_loc = group_idx * group
        start_tile = first_tile + offset_loc
        query_tile = lax.dynamic_slice_in_dim(query_tiles, offset_loc, group, 0)
        grad_tile = lax.dynamic_slice_in_dim(grad_tiles, offset_loc, group, 0)
        live = lax.dynamic_slice_in_dim(live_slot, offset_loc, group, 0)
        keys_sel = slab_stack(doubled_keys, start_tile, offsets, group, tile_total, slot_count)
        values_sel = slab_stack(doubled_values, start_tile, offsets, group, tile_total, slot_count)
        live_mask = live[:, None, None, :, None]
        scores = (
            jnp.einsum(
                "tqhd,stkhd->thqsk", query_tile, keys_sel, preferred_element_type=jnp.float32
            )
            * scaling
        )
        scores = jnp.where(live_mask, scores, -jnp.inf)
        row_top = jnp.max(scores, axis=(3, 4), keepdims=True)
        row_total = jnp.sum(jnp.exp(scores - row_top), axis=(3, 4), keepdims=True)
        log_total = row_top + jnp.log(row_total)
        prob_rows = jnp.exp(scores - log_total)
        weights = prob_rows.astype(jnp.bfloat16)
        attended = jnp.einsum(
            "thqsk,stkhd->tqhd", weights, values_sel, preferred_element_type=jnp.float32
        ).astype(jnp.bfloat16)
        row_delta = jnp.sum(attended.astype(jnp.float32) * grad_tile.astype(jnp.float32), axis=-1)
        dprob_rows = jnp.einsum(
            "tqhd,stkhd->thqsk", grad_tile, values_sel, preferred_element_type=jnp.float32
        )
        dscore = (
            prob_rows * (dprob_rows - row_delta.transpose(0, 2, 1)[:, :, :, None, None])
        ).astype(jnp.bfloat16)
        grad_query = (
            jnp.einsum("thqsk,stkhd->tqhd", dscore, keys_sel, preferred_element_type=jnp.float32)
            * scaling
        ).astype(jnp.bfloat16)
        return (
            start_tile,
            query_tile,
            grad_tile,
            attended,
            grad_query,
            log_total[:, :, :, 0, 0],
            row_delta,
            weights,
            dscore,
        )

    group_ids = jnp.arange(group_count, dtype=jnp.int32)

    def group_with_sums(carry, group_idx):
        key_acc, value_acc = carry
        (
            start_tile,
            query_tile,
            grad_tile,
            attended,
            grad_query,
            log_total,
            row_delta,
            weights,
            dscore,
        ) = forward_group(group_idx)
        key_part = jnp.einsum(
            "thqsk,tqhd->stkhd", dscore, query_tile, preferred_element_type=jnp.float32
        )
        value_part = jnp.einsum(
            "thqsk,tqhd->stkhd", weights, grad_tile, preferred_element_type=jnp.float32
        )
        key_acc = add_slabs(key_acc, key_part, start_tile, offsets, group, tile_total, slot_count)
        value_acc = add_slabs(
            value_acc, value_part, start_tile, offsets, group, tile_total, slot_count
        )
        return ((key_acc, value_acc), (attended, grad_query))

    zeros = jnp.zeros((2 * tile_total, BLOCK, heads_here, HEAD_DIM), jnp.float32)
    sums, outputs = lax.scan(group_with_sums, (zeros, zeros), group_ids)
    key_fold = sums[0][:tile_total] + sums[0][tile_total:]
    value_fold = sums[1][:tile_total] + sums[1][tile_total:]
    whole_rows = tile_total * BLOCK
    key_sum, value_sum = (
        lax.psum_scatter(
            key_fold.reshape(whole_rows, heads_here, HEAD_DIM).astype(jnp.bfloat16),
            "tm",
            scatter_dimension=0,
            tiled=True,
        ).astype(jnp.float32),
        lax.psum_scatter(
            value_fold.reshape(whole_rows, heads_here, HEAD_DIM).astype(jnp.bfloat16),
            "tm",
            scatter_dimension=0,
            tiled=True,
        ).astype(jnp.float32),
    )
    attended = outputs[0].reshape(tokens_here, heads_here, HEAD_DIM)
    grad_query = outputs[1].reshape(tokens_here, heads_here, HEAD_DIM)
    grad_key = (key_sum * scaling).astype(jnp.bfloat16)
    grad_value = value_sum.astype(jnp.bfloat16)
    width = heads_here * HEAD_DIM
    results = (
        lax.all_to_all(
            attended.reshape(tokens_here, width), "head", split_axis=0, concat_axis=1, tiled=True
        ),
        lax.all_to_all(
            grad_query.reshape(tokens_here, width), "head", split_axis=0, concat_axis=1, tiled=True
        ),
        lax.all_to_all(
            grad_key.reshape(tokens_here, width), "head", split_axis=0, concat_axis=1, tiled=True
        ),
        lax.all_to_all(
            grad_value.reshape(tokens_here, width), "head", split_axis=0, concat_axis=1, tiled=True
        ),
    )
    return (results[0], results[1], results[2], results[3])


def solution(mesh):
    in_specs = (
        P(("tm", "head"), None),
        P(("tm", "head"), None),
        P(("tm", "head"), None),
        P(("tm", "head"), None),
        P(),
    )
    out_specs = (
        P(("tm", "head"), None),
        P(("tm", "head"), None),
        P(("tm", "head"), None),
        P(("tm", "head"), None),
    )
    return jax.shard_map(
        on_device, mesh=mesh, in_specs=in_specs, out_specs=out_specs, check_vma=False
    )
```

profile of v0, /device:TPU:0, one launch (start us, length us, event | category | flops | bytes accessed | tf_op | source)
XLA Modules:
  0.0 907.8 jit_solution(187144626901690413)
XLA Ops:
  8.6 19.1 %all_to_all.140 = bf16[256,4,512]{2,0,1:T(8,128)(2,1)S(1)} all-to-all(bf16[256,4,512]{2,0,1:T(8,128)(2,1)S(1)} %bitcast.670), channel_id=1, replica_groups=mesh['tm'=8,'head'=4] {'head'}, dimensions={1} | all-to-all | bytes 2097152 | tf_op jit(solution)/shard_map/all_to_all | solution.py:34
  30.2 15.3 %all_to_all.141 = bf16[256,4,512]{2,0,1:T(8,128)(2,1)S(1)} all-to-all(bf16[256,4,512]{2,0,1:T(8,128)(2,1)S(1)} %bitcast.671), channel_id=1, replica_groups=mesh['tm'=8,'head'=4] {'head'}, dimensions={1} | all-to-all | bytes 2097152 | tf_op jit(solution)/shard_map/all_to_all | solution.py:33
  49.0 3.5 all-to-all-start
  53.6 10.2 %all-to-all-done = bf16[256,4,512]{2,0,1:T(8,128)(2,1)S(1)} async-done(((bf16[256,4,512]{2,0,1:T(8,128)(2,1)}), bf16[256,4,512]{2,0,1:T(8,128)(2,1)S(1)}, u32[]{:S(2)}, u32[]{:S(2)}) %all-to-all-start) | async-done | bytes 1048608 | tf_op jit(solution)/shard_map/all_to_all | solution.py:32
  63.7 3.5 all-to-all-start.2
  68.7 11.6 %all-to-all-done.2 = bf16[256,4,512]{2,0,1:T(8,128)(2,1)S(1)} async-done(((bf16[256,4,512]{2,0,1:T(8,128)(2,1)}), bf16[256,4,512]{2,0,1:T(8,128)(2,1)S(1)}, u32[]{:S(2)}, u32[]{:S(2)}) %all-to-all-start.2) | async-done | bytes 1048608 | tf_op jit(solution)/shard_map/all_to_all | solution.py:35
  81.4 29.4 %all-gather.5.cloned.1.call-done = bf16[8192,4,128]{2,1,0:T(4,128)(2,1)} async-done(((bf16[1024,4,128]{2,1,0:T(4,128)(2,1)}), bf16[8192,4,128]{2,1,0:T(4,128)(2,1)}) %all-gather.5.cloned.1.call-update) | async-done | bytes 8388624 | tf_op jit(solution)/shard_map/all_gather | solution.py:55
  110.8 7.7 copy.233
  118.5 8.6 pad_maximum_fusion.1
  127.1 7.1 copy.238
  134.3 59.4 %all-gather.3.cloned.1.call-done = bf16[8192,4,128]{2,1,0:T(4,128)(2,1)} async-done(((bf16[1024,4,128]{2,1,0:T(4,128)(2,1)}), bf16[8192,4,128]{2,1,0:T(4,128)(2,1)}) %all-gather.3.cloned.1.call-update) | async-done | bytes 8388624 | tf_op jit(solution)/shard_map/all_gather | solution.py:54
  193.6 7.7 copy.230
  201.3 8.3 pad_maximum_fusion
  209.6 7.2 copy.236
  216.7 11.2 %broadcast_in_dim.43.clone = f32[128,128,4,128]{1,3,2,0:T(8,128)} broadcast(f32[]{:T(128)} %constant.247.clone.1), dimensions={} | broadcast | bytes 33554436 | tf_op jit(solution)/shard_map/broadcast_in_dim | solution.py:138
  228.0 11.3 %broadcast_in_dim.43 = f32[128,128,4,128]{1,3,2,0:T(8,128)} broadcast(f32[]{:T(128)} %constant.247.clone.1), dimensions={} | broadcast | bytes 33554436 | tf_op jit(solution)/shard_map/broadcast_in_dim | solution.py:138
  239.2 412.3 %while.18 = (s32[]{:T(128)}, f32[128,128,4,128]{1,3,2,0:T(8,128)}, f32[128,128,4,128]{1,3,2,0:T(8,128)}, bf16[2,4,128,4,128]{4,3,2,1,0:T(4,128)(2,1)}, bf16[2,4,...) while((s32[]{:T(128)}, f32[128,128,4,128]{1,3,2,0:T(8,128)}, ...), condition=%wide.region_5.6_spmd, body=%wide.region_1.5_spmd.sunk | while | flops 6949433344 | bytes 604073728 | solution.py:139
  277.3 3.9 copy-done.1
  281.3 7.5 fusion.149
  288.8 10.0 %exponential_reduce_fusion.2 = f32[4,4,128]{2,1,0:T(4,128)S(1)} fusion(f32[4,4,128,17,128]{2,4,3,1,0:T(8,128)} %get-tuple-element.405, f32[4,4,128]{2,1,0:T(4,128)S(1)} %get-tuple-element.406, pred[4,17]{1,0:T(4,128)(4,1)S(1)} %constant_dynamic-slice_fusion.8), kind=kLoop, calls=%fused_computation.2.clone.1 | loop fusion | flops 17823744 | bytes 17842244 | tf_op jit(solution)/shard_map/while/body/eval_jaxpr/reduce_sum | solution.py:81
  298.8 11.2 %multiply_reduce_fusion.2 = (f32[4,128,4]{1,2,0:T(4,128)S(1)}, bf16[4,4,128,128]{2,3,1,0:T(8,128)(2,1)S(1)}) fusion(bf16[4,128,4,128]{3,2,1,0:T(4,128)(2,1)S(1)} %constant_dynamic-slice_fusion.7, bf16[17,4,128,4,128]{4,2,0,3,1:T(8,128)(2,1)} %copy-done.5, f32[4,4,128,17,128]{2,4,3,1,0:T(8,128)} %get-tuple-element.405, ...), kind=kOutput, calls=%fused_computation.116.clone.1 | convolution fusion | flops 1159985152 | bytes 27803716 | tf_op jit(solution)/shard_map/while/body/eval_jaxpr/thqsk,stkhd->tqhd/dot_general | solution.py:85
  310.1 14.0 %multiply_convert_fusion.3 = bf16[4,4,128,17,128]{2,4,3,1,0:T(8,128)(2,1)} fusion(f32[4,4,128,17,128]{2,4,3,1,0:T(8,128)} %get-tuple-element.405, f32[4,4,128]{2,1,0:T(4,128)S(1)} %bitcast.681, f32[4,4,128]{2,1,0:T(4,128)S(1)} %bitcast.678, pred[4,17]{1,0:T(4,128)(4,1)S(1)} %constant_dynamic-slice_fusion.8, ...), kind=kOutput, calls=%fused_computation.clone.1 | convolution fusion | flops 1167589376 | bytes 36192324 | tf_op jit(solution)/shard_map/while/body/eval_jaxpr/tqhd,stkhd->thqsk/dot_general | solution.py:89
  324.1 9.2 %fusion.183 = bf16[1,4,128,4,128]{2,4,3,1,0:T(8,128)(2,1)S(1)} fusion(bf16[17,4,128,4,128]{4,2,0,3,1:T(8,128)(2,1)} %copy-done.1, bf16[4,4,128,17,128]{2,4,3,1,0:T(8,128)(2,1)} %multiply_convert_fusion.3), kind=kOutput, calls=%fused_computation.13.clone.1 | convolution fusion | flops 1141374976 | bytes 18350080 | tf_op jit(solution)/shard_map/while/body/eval_jaxpr/thqsk,stkhd->tqhd/dot_general | solution.py:96
  333.3 11.9 %convolution_bitcast_fusion.6 = f32[17,4,128,4,128]{2,4,0,3,1:T(8,128)} fusion(bf16[4,128,4,128]{3,2,1,0:T(4,128)(2,1)S(1)} %constant_dynamic-slice_fusion.7, f32[4,4,128,17,128]{2,4,3,1,0:T(8,128)} %get-tuple-element.405, f32[4,4,128]{2,1,0:T(4,128)S(1)} %bitcast.679, pred[4,17]{1,0:T(4,128)(4,1)S(1)} %constant_dynamic-slice_fusion.8), kind=kOutput, calls=%fused_computation.6.clone.1 | convolution fusion | flops 1158676480 | bytes 36184132 | tf_op jit(solution)/shard_map/while/body/eval_jaxpr/thqsk,tqhd->stkhd/dot_general | solution.py:129
  347.1 12.7 %convolution_bitcast_fusion.7 = f32[17,4,128,4,128]{2,4,0,3,1:T(8,128)} fusion(bf16[4,4,128,17,128]{2,4,3,1,0:T(8,128)(2,1)} %multiply_convert_fusion.3, bf16[4,128,4,128]{3,2,1,0:T(4,128)(2,1)} %copy-done.3), kind=kOutput, calls=%fused_computation.7.clone.1 | convolution fusion | flops 1140850688 | bytes 27262976 | tf_op jit(solution)/shard_map/while/body/eval_jaxpr/thqsk,tqhd->stkhd/dot_general | solution.py:126
  359.8 4.0 fusion.150
  480.3 3.9 copy-done.1
  484.3 7.5 fusion.149
  491.8 10.0 %exponential_reduce_fusion.2 = f32[4,4,128]{2,1,0:T(4,128)S(1)} fusion(f32[4,4,128,17,128]{2,4,3,1,0:T(8,128)} %get-tuple-element.405, f32[4,4,128]{2,1,0:T(4,128)S(1)} %get-tuple-element.406, pred[4,17]{1,0:T(4,128)(4,1)S(1)} %constant_dynamic-slice_fusion.8), kind=kLoop, calls=%fused_computation.2.clone.1 | loop fusion | flops 17823744 | bytes 17842244 | tf_op jit(solution)/shard_map/while/body/eval_jaxpr/reduce_sum | solution.py:81
  501.9 11.2 %multiply_reduce_fusion.2 = (f32[4,128,4]{1,2,0:T(4,128)S(1)}, bf16[4,4,128,128]{2,3,1,0:T(8,128)(2,1)S(1)}) fusion(bf16[4,128,4,128]{3,2,1,0:T(4,128)(2,1)S(1)} %constant_dynamic-slice_fusion.7, bf16[17,4,128,4,128]{4,2,0,3,1:T(8,128)(2,1)} %copy-done.5, f32[4,4,128,17,128]{2,4,3,1,0:T(8,128)} %get-tuple-element.405, ...), kind=kOutput, calls=%fused_computation.116.clone.1 | convolution fusion | flops 1159985152 | bytes 27803716 | tf_op jit(solution)/shard_map/while/body/eval_jaxpr/thqsk,stkhd->tqhd/dot_general | solution.py:85
  513.1 14.0 %multiply_convert_fusion.3 = bf16[4,4,128,17,128]{2,4,3,1,0:T(8,128)(2,1)} fusion(f32[4,4,128,17,128]{2,4,3,1,0:T(8,128)} %get-tuple-element.405, f32[4,4,128]{2,1,0:T(4,128)S(1)} %bitcast.681, f32[4,4,128]{2,1,0:T(4,128)S(1)} %bitcast.678, pred[4,17]{1,0:T(4,128)(4,1)S(1)} %constant_dynamic-slice_fusion.8, ...), kind=kOutput, calls=%fused_computation.clone.1 | convolution fusion | flops 1167589376 | bytes 36192324 | tf_op jit(solution)/shard_map/while/body/eval_jaxpr/tqhd,stkhd->thqsk/dot_general | solution.py:89
  527.1 9.2 %fusion.183 = bf16[1,4,128,4,128]{2,4,3,1,0:T(8,128)(2,1)S(1)} fusion(bf16[17,4,128,4,128]{4,2,0,3,1:T(8,128)(2,1)} %copy-done.1, bf16[4,4,128,17,128]{2,4,3,1,0:T(8,128)(2,1)} %multiply_convert_fusion.3), kind=kOutput, calls=%fused_computation.13.clone.1 | convolution fusion | flops 1141374976 | bytes 18350080 | tf_op jit(solution)/shard_map/while/body/eval_jaxpr/thqsk,stkhd->tqhd/dot_general | solution.py:96
  536.3 11.9 %convolution_bitcast_fusion.6 = f32[17,4,128,4,128]{2,4,0,3,1:T(8,128)} fusion(bf16[4,128,4,128]{3,2,1,0:T(4,128)(2,1)S(1)} %constant_dynamic-slice_fusion.7, f32[4,4,128,17,128]{2,4,3,1,0:T(8,128)} %get-tuple-element.405, f32[4,4,128]{2,1,0:T(4,128)S(1)} %bitcast.679, pred[4,17]{1,0:T(4,128)(4,1)S(1)} %constant_dynamic-slice_fusion.8), kind=kOutput, calls=%fused_computation.6.clone.1 | convolution fusion | flops 1158676480 | bytes 36184132 | tf_op jit(solution)/shard_map/while/body/eval_jaxpr/thqsk,tqhd->stkhd/dot_general | solution.py:129
  550.1 12.7 %convolution_bitcast_fusion.7 = f32[17,4,128,4,128]{2,4,0,3,1:T(8,128)} fusion(bf16[4,4,128,17,128]{2,4,3,1,0:T(8,128)(2,1)} %multiply_convert_fusion.3, bf16[4,128,4,128]{3,2,1,0:T(4,128)(2,1)} %copy-done.3), kind=kOutput, calls=%fused_computation.7.clone.1 | convolution fusion | flops 1140850688 | bytes 27262976 | tf_op jit(solution)/shard_map/while/body/eval_jaxpr/thqsk,tqhd->stkhd/dot_general | solution.py:126
  562.8 4.0 fusion.150
  572.3 3.4 fusion.168
  651.5 31.2 %copy.243 = f32[128,128,4,128]{3,1,0,2:T(8,128)} copy(f32[128,128,4,128]{1,3,2,0:T(8,128)} %get-tuple-element.171) | data formatting | bytes 67108864 | tf_op jit(solution)/shard_map/while | solution.py:139
  682.7 15.2 %fusion.86 = bf16[64,128,4,128]{3,1,0,2:T(8,128)(2,1)} fusion(f32[128,128,4,128]{3,1,0,2:T(8,128)} %copy.243), kind=kLoop, calls=%fused_computation.170 | loop fusion | flops 8388608 | bytes 41943040 | tf_op jit(solution)/shard_map/convert_element_type | solution.py:145
  698.0 31.4 %copy.247 = f32[128,128,4,128]{3,1,0,2:T(8,128)} copy(f32[128,128,4,128]{1,3,2,0:T(8,128)} %get-tuple-element.172) | data formatting | bytes 67108864 | tf_op jit(solution)/shard_map/while | solution.py:139
  729.4 15.6 %fusion.85 = bf16[64,128,4,128]{3,1,0,2:T(8,128)(2,1)} fusion(f32[128,128,4,128]{3,1,0,2:T(8,128)} %copy.247), kind=kLoop, calls=%fused_computation.168 | loop fusion | flops 8388608 | bytes 41943040 | tf_op jit(solution)/shard_map/convert_element_type | solution.py:151
  747.3 3.7 all-to-all-start.5
  753.2 11.6 %all-to-all-done.5 = bf16[4,256,512]{2,1,0:T(8,128)(2,1)S(1)} async-done(((bf16[4,256,512]{2,1,0:T(8,128)(2,1)}), bf16[4,256,512]{2,1,0:T(8,128)(2,1)S(1)}, u32[]{:S(2)}, u32[]{:S(2)}) %all-to-all-start.5) | async-done | bytes 1048608 | tf_op jit(solution)/shard_map/all_to_all | solution.py:166
  764.8 3.5 all-to-all-start.4
  768.3 18.5 %reduce-scatter.3.cloned.1.call-done = bf16[1024,4,128]{2,0,1:T(8,128)(2,1)} async-done(((bf16[8192,4,128]{2,0,1:T(8,128)(2,1)}), bf16[1024,4,128]{2,0,1:T(8,128)(2,1)}) %reduce-scatter.3.cloned.1.call-update) | async-done | bytes 1048592 | tf_op jit(solution)/shard_map/reduce_scatter | solution.py:144
  790.2 3.7 all-to-all-start.6
  793.9 83.0 %reduce-scatter.5.cloned.1.call-done = bf16[1024,4,128]{2,0,1:T(8,128)(2,1)} async-done(((bf16[8192,4,128]{2,0,1:T(8,128)(2,1)}), bf16[1024,4,128]{2,0,1:T(8,128)(2,1)}) %reduce-scatter.5.cloned.1.call-update) | async-done | bytes 1048592 | tf_op jit(solution)/shard_map/reduce_scatter | solution.py:150
  882.1 4.2 all-to-all-start.7
  893.9 4.4 all-to-all-done.7
  (231 shorter events, 243.8 us)
Async XLA Ops:
  7.2 45.3 %copy-start.4 = (bf16[256,2048]{1,0:T(8,128)(2,1)S(1)}, bf16[256,2048]{1,0:T(8,128)(2,1)}, u32[]{:S(2)}) copy-start(bf16[256,2048]{1,0:T(8,128)(2,1)} %param.10) | copy-start | bytes 3145732
  7.2 60.1 %copy-start.6 = (s32[64,17]{0,1:T(8,128)S(1)}, s32[64,17]{0,1:T(8,128)}, u32[]{:S(2)}) copy-start(s32[64,17]{0,1:T(8,128)} %param.11) | copy-start | bytes 13060
  7.2 103.6 %all-gather.5.cloned.1.call-start = ((), (), s32[]{:S(2)}) async-start(), calls=%async_computation.11 | async-start | bytes 9437184 | tf_op jit(solution)/shard_map/all_gather | solution.py:55
  28.9 164.7 %all-gather.3.cloned.1.call-start = ((), (), s32[]{:S(2)}) async-start(), calls=%async_computation.10 | async-start | bytes 9437184 | tf_op jit(solution)/shard_map/all_gather | solution.py:54
  49.0 14.8 %all-to-all-start = ((bf16[256,4,512]{2,0,1:T(8,128)(2,1)}), bf16[256,4,512]{2,0,1:T(8,128)(2,1)S(1)}, u32[]{:S(2)}, u32[]{:S(2)}) async-start(bf16[256,4,512]{2,0,1:T(8,128)(2,1)} %bitcast.438), calls=%async_computation | async-start | bytes 2097152 | tf_op jit(solution)/shard_map/all_to_all | solution.py:32
  63.7 16.6 %all-to-all-start.2 = ((bf16[256,4,512]{2,0,1:T(8,128)(2,1)}), bf16[256,4,512]{2,0,1:T(8,128)(2,1)S(1)}, u32[]{:S(2)}, u32[]{:S(2)}) async-start(bf16[256,4,512]{2,0,1:T(8,128)(2,1)} %bitcast.436), calls=%async_computation.2 | async-start | bytes 2097152 | tf_op jit(solution)/shard_map/all_to_all | solution.py:35
  67.2 719.5 %reduce-scatter.3.cloned.1.call-start = ((), (), s32[]{:S(2)}) async-start(), calls=%async_computation.12 | async-start | bytes 9437184 | tf_op jit(solution)/shard_map/reduce_scatter | solution.py:144
  252.5 23.2 %copy-start.2 = (bf16[128,128,4,128]{3,1,2,0:T(8,128)(2,1)S(1)}, bf16[128,128,4,128]{3,1,2,0:T(8,128)(2,1)}, u32[]{:S(2)}) copy-start(bf16[128,128,4,128]{3,1,2,0:T(8,128)(2,1)} %get-tuple-element.463) | copy-start | bytes 50331652 | tf_op jit(solution)/shard_map/while
  255.4 21.9 %copy-start.3 = (bf16[4,128,4,128]{3,2,1,0:T(4,128)(2,1)}, bf16[4,128,4,128]{3,2,1,0:T(4,128)(2,1)S(1)}, u32[]{:S(2)}) copy-start(bf16[4,128,4,128]{3,2,1,0:T(4,128)(2,1)S(1)} %constant_dynamic-slice_fusion.9) | copy-start | bytes 1572868 | tf_op jit(solution)/shard_map/while
  275.7 13.1 %copy-start.5 = (bf16[17,4,128,4,128]{4,2,0,3,1:T(8,128)(2,1)}, bf16[17,4,128,4,128]{4,2,0,3,1:T(8,128)(2,1)S(1)}, u32[]{:S(2)}) copy-start(bf16[17,4,128,4,128]{4,2,0,3,1:T(8,128)(2,1)S(1)} %bitcast_dynamic-update-slice_fusion.101) | copy-start | bytes 26738692 | tf_op jit(solution)/shard_map/while
  277.3 4.0 copy-start.1
  347.1 31.7 %slice-start = ((s8[17825792]{0:T(1024)(128)(4,1)}), s8[4194304]{0:T(1024)(128)(4,1)S(1)}, s32[]{:S(2)}) async-start(s8[17825792]{0:T(1024)(128)(4,1)} %bitcast.652), calls=%async_computation.14 | async-start | bytes 8388608 | tf_op jit(solution)/shard_map/while
  347.1 31.7 %slice-start.1 = ((s8[17825792]{0:T(1024)(128)(4,1)}), s8[4194304]{0:T(1024)(128)(4,1)S(1)}, s32[]{:S(2)}) async-start(s8[17825792]{0:T(1024)(128)(4,1)} %bitcast.652), calls=%async_computation.15 | async-start | bytes 8388608 | tf_op jit(solution)/shard_map/while
  347.1 31.7 %slice-start.2 = ((s8[17825792]{0:T(1024)(128)(4,1)}), s8[1048576]{0:T(1024)(128)(4,1)S(1)}, s32[]{:S(2)}) async-start(s8[17825792]{0:T(1024)(128)(4,1)} %bitcast.652), calls=%async_computation.16 | async-start | bytes 2097152 | tf_op jit(solution)/shard_map/while
  359.8 19.0 %slice-start.3 = ((s8[17825792]{0:T(1024)(128)(4,1)}), s8[4194304]{0:T(1024)(128)(4,1)S(1)}, s32[]{:S(2)}) async-start(s8[17825792]{0:T(1024)(128)(4,1)} %bitcast.652), calls=%async_computation.17 | async-start | bytes 8388608 | tf_op jit(solution)/shard_map/while
  366.5 12.4 %slice-start.4 = ((s8[17825792]{0:T(1024)(128)(4,1)}), s8[4194304]{0:T(1024)(128)(4,1)S(1)}, s32[]{:S(2)}) async-start(s8[17825792]{0:T(1024)(128)(4,1)} %bitcast.652), calls=%async_computation.18 | async-start | bytes 8388608 | tf_op jit(solution)/shard_map/while
  366.5 19.8 %copy-start = (f32[17,4,128,4,128]{2,4,0,3,1:T(8,128)S(1)}, f32[17,4,128,4,128]{2,4,0,3,1:T(8,128)}, u32[]{:S(2)}) copy-start(f32[17,4,128,4,128]{2,4,0,3,1:T(8,128)} %convolution_bitcast_fusion.7) | copy-start | bytes 53477380 | tf_op jit(solution)/shard_map/while
  455.5 23.2 %copy-start.2 = (bf16[128,128,4,128]{3,1,2,0:T(8,128)(2,1)S(1)}, bf16[128,128,4,128]{3,1,2,0:T(8,128)(2,1)}, u32[]{:S(2)}) copy-start(bf16[128,128,4,128]{3,1,2,0:T(8,128)(2,1)} %get-tuple-element.463) | copy-start | bytes 50331652 | tf_op jit(solution)/shard_map/while
  458.4 21.9 %copy-start.3 = (bf16[4,128,4,128]{3,2,1,0:T(4,128)(2,1)}, bf16[4,128,4,128]{3,2,1,0:T(4,128)(2,1)S(1)}, u32[]{:S(2)}) copy-start(bf16[4,128,4,128]{3,2,1,0:T(4,128)(2,1)S(1)} %constant_dynamic-slice_fusion.9) | copy-start | bytes 1572868 | tf_op jit(solution)/shard_map/while
  478.7 13.1 %copy-start.5 = (bf16[17,4,128,4,128]{4,2,0,3,1:T(8,128)(2,1)}, bf16[17,4,128,4,128]{4,2,0,3,1:T(8,128)(2,1)S(1)}, u32[]{:S(2)}) copy-start(bf16[17,4,128,4,128]{4,2,0,3,1:T(8,128)(2,1)S(1)} %bitcast_dynamic-update-slice_fusion.101) | copy-start | bytes 26738692 | tf_op jit(solution)/shard_map/while
  480.3 4.0 copy-start.1
  550.1 31.7 %slice-start = ((s8[17825792]{0:T(1024)(128)(4,1)}), s8[4194304]{0:T(1024)(128)(4,1)S(1)}, s32[]{:S(2)}) async-start(s8[17825792]{0:T(1024)(128)(4,1)} %bitcast.652), calls=%async_computation.14 | async-start | bytes 8388608 | tf_op jit(solution)/shard_map/while
  550.1 31.7 %slice-start.1 = ((s8[17825792]{0:T(1024)(128)(4,1)}), s8[4194304]{0:T(1024)(128)(4,1)S(1)}, s32[]{:S(2)}) async-start(s8[17825792]{0:T(1024)(128)(4,1)} %bitcast.652), calls=%async_computation.15 | async-start | bytes 8388608 | tf_op jit(solution)/shard_map/while
  550.1 31.7 %slice-start.2 = ((s8[17825792]{0:T(1024)(128)(4,1)}), s8[1048576]{0:T(1024)(128)(4,1)S(1)}, s32[]{:S(2)}) async-start(s8[17825792]{0:T(1024)(128)(4,1)} %bitcast.652), calls=%async_computation.16 | async-start | bytes 2097152 | tf_op jit(solution)/shard_map/while
  562.8 19.0 %slice-start.3 = ((s8[17825792]{0:T(1024)(128)(4,1)}), s8[4194304]{0:T(1024)(128)(4,1)S(1)}, s32[]{:S(2)}) async-start(s8[17825792]{0:T(1024)(128)(4,1)} %bitcast.652), calls=%async_computation.17 | async-start | bytes 8388608 | tf_op jit(solution)/shard_map/while
  569.5 12.3 %slice-start.4 = ((s8[17825792]{0:T(1024)(128)(4,1)}), s8[4194304]{0:T(1024)(128)(4,1)S(1)}, s32[]{:S(2)}) async-start(s8[17825792]{0:T(1024)(128)(4,1)} %bitcast.652), calls=%async_computation.18 | async-start | bytes 8388608 | tf_op jit(solution)/shard_map/while
  569.5 19.7 %copy-start = (f32[17,4,128,4,128]{2,4,0,3,1:T(8,128)S(1)}, f32[17,4,128,4,128]{2,4,0,3,1:T(8,128)}, u32[]{:S(2)}) copy-start(f32[17,4,128,4,128]{2,4,0,3,1:T(8,128)} %convolution_bitcast_fusion.7) | copy-start | bytes 53477380 | tf_op jit(solution)/shard_map/while
  697.9 178.9 %reduce-scatter.5.cloned.1.call-start = ((), (), s32[]{:S(2)}) async-start(), calls=%async_computation.13 | async-start | bytes 9437184 | tf_op jit(solution)/shard_map/reduce_scatter | solution.py:150
  747.3 17.5 %all-to-all-start.5 = ((bf16[4,256,512]{2,1,0:T(8,128)(2,1)}), bf16[4,256,512]{2,1,0:T(8,128)(2,1)S(1)}, u32[]{:S(2)}, u32[]{:S(2)}) async-start(bf16[4,256,512]{2,1,0:T(8,128)(2,1)} %all_to_all.120), calls=%async_computation.5 | async-start | bytes 2097152 | tf_op jit(solution)/shard_map/all_to_all | solution.py:166
  764.8 25.5 %all-to-all-start.4 = ((bf16[4,256,512]{2,1,0:T(8,128)(2,1)}), bf16[4,256,512]{2,1,0:T(8,128)(2,1)S(1)}, u32[]{:S(2)}, u32[]{:S(2)}) async-start(bf16[4,256,512]{2,1,0:T(8,128)(2,1)} %all_to_all.116), calls=%async_computation.4 | async-start | bytes 2097152 | tf_op jit(solution)/shard_map/all_to_all | solution.py:163
  790.2 91.9 %all-to-all-start.6 = ((bf16[4,256,512]{2,1,0:T(8,128)(2,1)}), bf16[4,256,512]{2,1,0:T(8,128)(2,1)S(1)}, u32[]{:S(2)}, u32[]{:S(2)}) async-start(bf16[4,256,512]{2,1,0:T(8,128)(2,1)} %all_to_all.124), calls=%async_computation.7 | async-start | bytes 2097152 | tf_op jit(solution)/shard_map/all_to_all | solution.py:169
  882.1 16.1 %all-to-all-start.7 = ((bf16[4,256,512]{2,1,0:T(8,128)(2,1)}), bf16[4,256,512]{2,1,0:T(8,128)(2,1)}, u32[]{:S(2)}, u32[]{:S(2)}) async-start(bf16[4,256,512]{2,1,0:T(8,128)(2,1)} %all_to_all.128), calls=%async_computation.9 | async-start | bytes 2097152 | tf_op jit(solution)/shard_map/all_to_all | solution.py:172
Sparse Core Ops, SparseCore 0:
  29.0 81.7 all-gather.4
  113.0 80.5 all-gather.2
  698.1 88.6 reduce-scatter.2
  788.9 87.9 reduce-scatter.4
where the time goes:
time: 924 us; the launch traced here: 908 us
  other arithmetic  235 us (25%)
  waiting for transfers between devices  228 us (25%)
  local copies, waits for them, and re-layouts  211 us (23%)
  matrix products  133 us (14%)
  blocking collectives  34.4 us (4%)
  loops' own time  30.5 us (3%)
  starting transfers between devices  22.3 us (2%)
  between operations  14.1 us (2%)
    dynamic_update_slice x66, other arithmetic, add_slabs(): lax.dynamic_update_slice_in_dim(accum, current + parts[slot], where_at, 0)  165 us
    reduce_scatter x1, waiting for transfers between devices, on_device(): lax.psum_scatter(value_fold.reshape(whole_rows, heads_here, HEAD_DIM).ast...  83 us
    while x4, local copies, waits for them, and re-layouts, on_device(): sums, outputs = lax.scan(group_with_sums, (zeros, zeros), group_ids)  76.8 us
    all_gather x1, waiting for transfers between devices, on_device(): lax.all_gather(key_loc, 'tm', axis=0, tiled=True)  59.4 us
    while x104, local copies, waits for them, and re-layouts  48.7 us
    another operation x1, loops' own time, on_device(): sums, outputs = lax.scan(group_with_sums, (zeros, zeros), group_ids)  30.5 us
    all_gather x1, waiting for transfers between devices, on_device(): lax.all_gather(value_loc, 'tm', axis=0, tiled=True)  29.4 us
    dot_general x2, matrix products, forward_group(): jnp.einsum('tqhd,stkhd->thqsk', grad_tile, values_sel, preferred_element_...  28 us
  transfers between devices with their start and end apart: 10, of which 8 were waited for; matrix products, arithmetic and copies ran while one was open for 10% of the time, Pallas kernels for 0%

commit v1 on v0

--- a/solution.py
+++ b/solution.py
@@ -1,13 +1,21 @@
+import functools
 import math
 
 import jax
 import jax.numpy as jnp
 from jax import lax
+from jax.experimental import pallas as pl
+from jax.experimental.pallas import tpu as pltpu
 from jax.sharding import PartitionSpec as P
 
 HEAD_DIM = 128
 HEADS = 16
 BLOCK = 128
+CHUNK = 4
+PAIR = 2
+DEPTHS = 5
+MESH = pl.DeviceIdType.MESH
+MIB = 1024 * 1024
 
 
 def slab_stack(doubled, start_tile, offsets, group, tile_total, slot_count):
@@ -176,6 +184,482 @@
     return (results[0], results[1], results[2], results[3])
 
 
+def place(pos, core, z_size):
+    return (2 * lax.rem(pos, z_size) + core, lax.div(pos, z_size))
+
+
+def slot_of(pos, z_size, hd_size):
+    return lax.rem(pos, z_size) * hd_size + lax.div(pos, z_size)
+
+
+def columns_of(pos):
+    return pl.ds(pl.multiple_of(pos * HEAD_DIM, HEAD_DIM), HEAD_DIM)
+
+
+def block_rows(index, rows):
+    return pl.ds(pl.multiple_of(index * rows, rows), rows)
+
+
+def greet(count, pos, core, z_size, tm, hd):
+    barrier = pltpu.get_barrier_semaphore()
+
+    def signal(step, carry):
+        other = lax.rem(pos + step, count)
+        pl.semaphore_signal(
+            barrier, inc=1, device_id=place(other, core, z_size), device_id_type=MESH
+        )
+        return carry
+
+    lax.fori_loop(1, count, signal, 0)
+    pl.semaphore_signal(
+        barrier, inc=1, device_id=(tm + 1 - 2 * core, hd), device_id_type=MESH
+    )
+    pl.semaphore_wait(barrier, count)
+
+
+def scatter_kernel(
+    tm_size, hd_size, q_ref, k_ref, v_ref, g_ref, qg_ref, kv_ref,
+    send, recv, pair_send, pair_recv, own_sem,
+):
+    z_size = tm_size // 2
+    count = z_size * hd_size
+    rows = q_ref.shape[0]
+    tm, hd = lax.axis_index("tm"), lax.axis_index("head")
+    core = lax.rem(tm, 2)
+    pos = hd * z_size + lax.div(tm, 2)
+    sibling = (tm + 1 - 2 * core, hd)
+    greet(count, pos, core, z_size, tm, hd)
+
+    left, right = pl.ds(0, HEAD_DIM), pl.ds(HEAD_DIM, HEAD_DIM)
+    sources = (k_ref, v_ref, q_ref, g_ref)
+
+    def global_block(where):
+        tm_of, hd_of = place(where, core, z_size)
+        return tm_of * hd_size + hd_of
+
+    def landing(tensor, where):
+        half = left if tensor % 2 == 0 else right
+        if tensor < 2:
+            return kv_ref.at[block_rows(global_block(where), rows), half]
+        return qg_ref.at[block_rows(slot_of(where, z_size, hd_size), rows), half]
+
+    def outgoing(tensor, target):
+        return pltpu.make_async_remote_copy(
+            src_ref=sources[tensor].at[:, columns_of(target)],
+            dst_ref=landing(tensor, pos),
+            send_sem=send.at[tensor, target],
+            recv_sem=recv.at[tensor, pos],
+            device_id=place(target, core, z_size),
+            device_id_type=MESH,
+        )
+
+    def incoming(tensor, origin):
+        return pltpu.make_async_remote_copy(
+            src_ref=sources[tensor].at[:, columns_of(pos)],
+            dst_ref=landing(tensor, origin),
+            send_sem=send.at[tensor, origin],
+            recv_sem=recv.at[tensor, origin],
+            device_id=place(origin, core, z_size),
+            device_id_type=MESH,
+        )
+
+    def to_sibling(where):
+        block = kv_ref.at[block_rows(global_block(where), rows), :]
+        return pltpu.make_async_remote_copy(
+            src_ref=block, dst_ref=block,
+            send_sem=pair_send.at[where], recv_sem=pair_recv.at[where],
+            device_id=sibling, device_id_type=MESH,
+        )
+
+    def from_sibling(where):
+        tm_of, hd_of = place(where, 1 - core, z_size)
+        block = kv_ref.at[block_rows(tm_of * hd_size + hd_of, rows), :]
+        return pltpu.make_async_remote_copy(
+            src_ref=block, dst_ref=block,
+            send_sem=pair_send.at[where], recv_sem=pair_recv.at[where],
+            device_id=sibling, device_id_type=MESH,
+        )
+
+    def send_pair(first):
+        def step_body(step, carry):
+            target = lax.rem(pos + step, count)
+            outgoing(first, target).start()
+            outgoing(first + 1, target).start()
+            return carry
+
+        lax.fori_loop(1, count, step_body, 0)
+
+    own = [
+        pltpu.make_async_copy(
+            sources[tensor].at[:, columns_of(pos)],
+            landing(tensor, pos),
+            own_sem.at[tensor],
+        )
+        for tensor in range(4)
+    ]
+    for copy in own:
+        copy.start()
+    send_pair(0)
+    send_pair(2)
+    own[0].wait()
+    own[1].wait()
+    to_sibling(pos).start()
+
+    def forward(step, carry):
+        origin = lax.rem(pos + count - step, count)
+        incoming(0, origin).wait_recv()
+        incoming(1, origin).wait_recv()
+        to_sibling(origin).start()
+        return carry
+
+    lax.fori_loop(1, count, forward, 0)
+    own[2].wait()
+    own[3].wait()
+
+    def finish(step, carry):
+        other = lax.rem(pos + count - step, count)
+        incoming(2, other).wait_recv()
+        incoming(3, other).wait_recv()
+        for tensor in range(4):
+            outgoing(tensor, other).wait_send()
+        return carry
+
+    lax.fori_loop(1, count, finish, 0)
+
+    def finish_pair(where, carry):
+        from_sibling(where).wait_recv()
+        to_sibling(where).wait_send()
+        return carry
+
+    lax.fori_loop(0, count, finish_pair, 0)
+
+
+def return_kernel(
+    tm_size, hd_size, o_ref, dq_ref, mine_ref, theirs_ref,
+    o_out, dq_out, dk_out, dv_out,
+    landed, total, send, recv, pair_send, pair_recv, own_sem,
+):
+    z_size = tm_size // 2
+    count = z_size * hd_size
+    rows = o_out.shape[0]
+    tm, hd = lax.axis_index("tm"), lax.axis_index("head")
+    core = lax.rem(tm, 2)
+    pos = hd * z_size + lax.div(tm, 2)
+    sibling = (tm + 1 - 2 * core, hd)
+    greet(count, pos, core, z_size, tm, hd)
+
+    left, right = pl.ds(0, HEAD_DIM), pl.ds(HEAD_DIM, HEAD_DIM)
+    outs = (o_out, dq_out, dv_out, dk_out)
+
+    def source(tensor, where):
+        if tensor < 2:
+            return (o_ref, dq_ref)[tensor].at[block_rows(slot_of(where, z_size, hd_size), rows), :]
+        return total.at[block_rows(slot_of(where, z_size, hd_size), rows), left if tensor == 2 else right]
+
+    def outgoing(tensor, target):
+        return pltpu.make_async_remote_copy(
+            src_ref=source(tensor, target),
+            dst_ref=outs[tensor].at[:, columns_of(pos)],
+            send_sem=send.at[tensor, target],
+            recv_sem=recv.at[tensor, pos],
+            device_id=place(target, core, z_size),
+            device_id_type=MESH,
+        )
+
+    def incoming(tensor, origin):
+        return pltpu.make_async_remote_copy(
+            src_ref=source(tensor, origin),
+            dst_ref=outs[tensor].at[:, columns_of(origin)],
+            send_sem=send.at[tensor, origin],
+            recv_sem=recv.at[tensor, origin],
+            device_id=place(origin, core, z_size),
+            device_id_type=MESH,
+        )
+
+    def pair(where):
+        return pltpu.make_async_remote_copy(
+            src_ref=theirs_ref.at[block_rows(slot_of(where, z_size, hd_size), rows), :],
+            dst_ref=landed.at[block_rows(slot_of(where, z_size, hd_size), rows), :],
+            send_sem=pair_send.at[where], recv_sem=pair_recv.at[where],
+            device_id=sibling, device_id_type=MESH,
+        )
+
+    def own(tensor):
+        return pltpu.make_async_copy(
+            source(tensor, pos),
+            outs[tensor].at[:, columns_of(pos)],
+            own_sem.at[tensor],
+        )
+
+    def start_pair(step, carry):
+        pair(lax.rem(pos + step, count)).start()
+        return carry
+
+    lax.fori_loop(1, count + 1, start_pair, 0)
+
+    def start_first(step, carry):
+        target = lax.rem(pos + step, count)
+        outgoing(0, target).start()
+        outgoing(1, target).start()
+        return carry
+
+    lax.fori_loop(1, count, start_first, 0)
+    own(0).start()
+    own(1).start()
+
+    def add(where):
+        pair(where).wait_recv()
+        here = block_rows(slot_of(where, z_size, hd_size), rows)
+        total[here, :] = (mine_ref[here, :] + landed[here, :].astype(jnp.float32)).astype(
+            jnp.bfloat16
+        )
+
+    def start_second(step, carry):
+        target = lax.rem(pos + step, count)
+        add(target)
+        outgoing(2, target).start()
+        outgoing(3, target).start()
+        return carry
+
+    lax.fori_loop(1, count, start_second, 0)
+    add(pos)
+    own(2).start()
+    own(3).start()
+    for tensor in range(4):
+        own(tensor).wait()
+
+    def finish(step, carry):
+        other = lax.rem(pos + count - step, count)
+        for tensor in range(4):
+            incoming(tensor, other).wait_recv()
+            outgoing(tensor, other).wait_send()
+        return carry
+
+    lax.fori_loop(1, count, finish, 0)
+
+    def finish_pair(where, carry):
+        pair(where).wait_send()
+        return carry
+
+    lax.fori_loop(0, count, finish_pair, 0)
+
+
+def attend_kernel(
+    tiles_per_shard, slots, lists_ref, counts_ref, core_ref, qg_ref, kv_ref,
+    o_ref, dq_ref, mine_ref, theirs_ref,
+    kv_t, scores, sums, read_w, sum_w,
+):
+    scaling = HEAD_DIM ** (-0.5)
+    step = pl.program_id(0)
+    tile_total = kv_ref.shape[0] // BLOCK
+
+    @pl.when(step == 0)
+    def _():
+        def turn(tile, carry):
+            kv_t[:, block_rows(tile, BLOCK)] = kv_ref[block_rows(tile, BLOCK), :].T
+            sums[block_rows(tile, BLOCK), :] = jnp.zeros((BLOCK, 2 * HEAD_DIM), jnp.float32)
+            return carry
+
+        lax.fori_loop(0, tile_total, turn, 0)
+        read_w[...] = jnp.zeros_like(read_w)
+        sum_w[...] = jnp.zeros_like(sum_w)
+
+    live = [counts_ref[step * PAIR + sub] for sub in range(PAIR)]
+    most = live[0]
+    for sub in range(1, PAIR):
+        most = jnp.maximum(most, live[sub])
+    rate = scaling * math.log2(math.e)
+
+    def read(sub, depth):
+        rows = slice(sub * BLOCK, (sub + 1) * BLOCK)
+        query, grad = qg_ref[rows, :HEAD_DIM], qg_ref[rows, HEAD_DIM:]
+        read_w[sub, :BLOCK, :HEAD_DIM] = query
+        read_w[sub, BLOCK:, HEAD_DIM:] = grad
+        sum_w[sub, :BLOCK, :HEAD_DIM] = grad
+        sum_w[sub, BLOCK:, HEAD_DIM:] = query
+        base = (step * PAIR + sub) * slots
+        tiles = [lists_ref[base + j] for j in range(depth)]
+        top = jnp.full((8, BLOCK), -jnp.inf, jnp.float32)
+        for first in range(0, depth, CHUNK):
+            group = tiles[first : first + CHUNK]
+            picked = jnp.concatenate([kv_ref[block_rows(t, BLOCK), :] for t in group], 0)
+            both = lax.dot_general(
+                picked, read_w[sub], (((1,), (1,)), ((), ())), preferred_element_type=jnp.float32
+            )
+            for j in range(len(group)):
+                bias = jnp.where(first + j < live[sub], 0.0, -jnp.inf).astype(jnp.float32)
+                part = both[j * BLOCK : (j + 1) * BLOCK, :BLOCK] + bias
+                here = slice((first + j) * BLOCK, (first + j + 1) * BLOCK)
+                scores[sub, here, :BLOCK] = part
+                scores[sub, here, BLOCK:] = both[j * BLOCK : (j + 1) * BLOCK, BLOCK:]
+                top = jnp.maximum(top, jnp.max(part.reshape(BLOCK // 8, 8, BLOCK), axis=0))
+        return tiles, jnp.max(top, axis=0, keepdims=True)
+
+    def weigh(sub, depth, tiles, top):
+        total = jnp.zeros((8, BLOCK), jnp.float32)
+        out_t = jnp.zeros((HEAD_DIM, BLOCK), jnp.float32)
+        for first in range(0, depth, CHUNK):
+            group = tiles[first : first + CHUNK]
+            here = slice(first * BLOCK, (first + len(group)) * BLOCK)
+            weight = jnp.exp2((scores[sub, here, :BLOCK] - top) * rate)
+            scores[sub, here, :BLOCK] = weight
+            total = total + jnp.sum(weight.reshape(-1, 8, BLOCK), axis=0)
+            values_t = jnp.concatenate([kv_t[HEAD_DIM:, block_rows(t, BLOCK)] for t in group], 1)
+            out_t = out_t + jnp.dot(
+                values_t, weight.astype(jnp.bfloat16), preferred_element_type=jnp.float32
+            )
+        inverse = 1.0 / jnp.sum(total, axis=0, keepdims=True)
+        out_t = (out_t * inverse).astype(jnp.bfloat16).astype(jnp.float32)
+        rows = slice(sub * BLOCK, (sub + 1) * BLOCK)
+        o_ref[rows, :] = out_t.T.astype(jnp.bfloat16)
+        grad_t = qg_ref[rows, HEAD_DIM:].astype(jnp.float32).T
+        return inverse, jnp.sum(out_t * grad_t, axis=0, keepdims=True)
+
+    def gather_sums(sub, depth, tiles, inverse, delta):
+        dq_t = jnp.zeros((HEAD_DIM, BLOCK), jnp.float32)
+        for first in range(0, depth, CHUNK):
+            group = tiles[first : first + CHUNK]
+            here = slice(first * BLOCK, (first + len(group)) * BLOCK)
+            prob = scores[sub, here, :BLOCK] * inverse
+            dscore = (prob * (scores[sub, here, BLOCK:] - delta)).astype(jnp.bfloat16)
+            both = jnp.concatenate([prob.astype(jnp.bfloat16), dscore], 1)
+            parts = jnp.dot(both, sum_w[sub], preferred_element_type=jnp.float32)
+            for j, tile in enumerate(group):
+                sums[block_rows(tile, BLOCK), :] += parts[j * BLOCK : (j + 1) * BLOCK, :]
+            keys_t = jnp.concatenate([kv_t[:HEAD_DIM, block_rows(t, BLOCK)] for t in group], 1)
+            dq_t = dq_t + jnp.dot(keys_t, dscore, preferred_element_type=jnp.float32)
+        rows = slice(sub * BLOCK, (sub + 1) * BLOCK)
+        dq_ref[rows, :] = (dq_t * scaling).T.astype(jnp.bfloat16)
+
+    def whole_pass(depth):
+        found = [read(sub, depth) for sub in range(PAIR)]
+        scales = [weigh(sub, depth, *found[sub]) for sub in range(PAIR)]
+        for sub in range(PAIR):
+            gather_sums(sub, depth, found[sub][0], *scales[sub])
+
+    depths = sorted({slots - 2 * k for k in range(DEPTHS) if slots - 2 * k > 0})
+    for k, depth in enumerate(depths):
+        above = depths[k - 1] if k else 0
+
+        @pl.when((most > above) & (most <= depth))
+        def _(depth=depth):
+            whole_pass(depth)
+
+    @pl.when(step == pl.num_programs(0) - 1)
+    def _():
+        core = core_ref[0]
+
+        def store(local, carry):
+            shard = lax.div(local, tiles_per_shard) * 2
+            within = lax.rem(local, tiles_per_shard)
+            here = block_rows(local, BLOCK)
+            mine = sums[block_rows((shard + core) * tiles_per_shard + within, BLOCK), :]
+            other = sums[block_rows((shard + 1 - core) * tiles_per_shard + within, BLOCK), :]
+            mine_ref[here, :HEAD_DIM] = mine[:, :HEAD_DIM]
+            mine_ref[here, HEAD_DIM:] = mine[:, HEAD_DIM:] * scaling
+            theirs_ref[here, :HEAD_DIM] = other[:, :HEAD_DIM].astype(jnp.bfloat16)
+            theirs_ref[here, HEAD_DIM:] = (other[:, HEAD_DIM:] * scaling).astype(jnp.bfloat16)
+            return carry
+
+        lax.fori_loop(0, pl.num_programs(0) * PAIR, store, 0)
+
+
+def on_pairs(queries, key_rows, value_rows, grad_out, tile_lists):
+    tm_size, hd_size = lax.axis_size("tm"), lax.axis_size("head")
+    count = tm_size // 2 * hd_size
+    rows, width = queries.shape
+    tile_total, slot_count = tile_lists.shape
+    tiles_here = tile_total // 2
+    tiles_per_shard = tile_total // tm_size
+    half = count * rows
+    bf16 = jnp.bfloat16
+    anywhere = pl.BlockSpec(memory_space=pl.ANY)
+    whole = pl.BlockSpec(memory_space=pltpu.VMEM)
+    dma = pltpu.SemaphoreType.DMA
+    qg, kv = pl.pallas_call(
+        functools.partial(scatter_kernel, tm_size, hd_size),
+        out_shape=(
+            jax.ShapeDtypeStruct((half, 2 * HEAD_DIM), bf16),
+            jax.ShapeDtypeStruct((2 * half, 2 * HEAD_DIM), bf16),
+        ),
+        in_specs=[anywhere] * 4,
+        out_specs=(anywhere, anywhere),
+        scratch_shapes=[
+            dma((4, count)), dma((4, count)), dma((count,)), dma((count,)), dma((4,)),
+        ],
+        compiler_params=pltpu.CompilerParams(collective_id=0, has_side_effects=True),
+        name="scatter_heads",
+    )(queries, key_rows, value_rows, grad_out)
+
+    core = lax.rem(lax.axis_index("tm"), 2)
+    own_lists = jnp.where(
+        core == 0,
+        tile_lists.reshape(tm_size // 2, 2, tiles_per_shard, slot_count)[:, 0],
+        tile_lists.reshape(tm_size // 2, 2, tiles_per_shard, slot_count)[:, 1],
+    ).reshape(tiles_here, slot_count)
+    live = own_lists >= 0
+    slots = slot_count
+    earlier = jnp.arange(slot_count)[:, None] <= jnp.arange(slot_count)[None, :]
+    rank = jnp.sum(jnp.where(live[:, :, None] & earlier[None], 1, 0), axis=1) - 1
+    hit = live[:, :, None] & (rank[:, :, None] == jnp.arange(slots)[None, None, :])
+    lists = jnp.sum(jnp.where(hit, own_lists[:, :, None], 0), axis=1).astype(jnp.int32)
+    counts = jnp.sum(live.astype(jnp.int32), axis=1)
+
+    tile_spec = pl.BlockSpec((PAIR * BLOCK, HEAD_DIM), lambda i, *_: (i, 0))
+    fixed = lambda i, *_: (0, 0)
+    o, dq, mine, theirs = pl.pallas_call(
+        functools.partial(attend_kernel, tiles_per_shard, slots),
+        grid_spec=pltpu.PrefetchScalarGridSpec(
+            num_scalar_prefetch=3,
+            grid=(tiles_here // PAIR,),
+            in_specs=[
+                pl.BlockSpec((PAIR * BLOCK, 2 * HEAD_DIM), lambda i, *_: (i, 0)),
+                pl.BlockSpec((2 * half, 2 * HEAD_DIM), fixed, pipeline_mode=pl.Buffered(1)),
+            ],
+            out_specs=(
+                tile_spec,
+                tile_spec,
+                pl.BlockSpec((half, 2 * HEAD_DIM), fixed),
+                pl.BlockSpec((half, 2 * HEAD_DIM), fixed),
+            ),
+            scratch_shapes=[
+                pltpu.VMEM((2 * HEAD_DIM, 2 * half), bf16),
+                pltpu.VMEM((PAIR, slots * BLOCK, 2 * BLOCK), jnp.float32),
+                pltpu.VMEM((2 * half, 2 * HEAD_DIM), jnp.float32),
+                pltpu.VMEM((PAIR, 2 * BLOCK, 2 * HEAD_DIM), bf16),
+                pltpu.VMEM((PAIR, 2 * BLOCK, 2 * HEAD_DIM), bf16),
+            ],
+        ),
+        out_shape=(
+            jax.ShapeDtypeStruct((half, HEAD_DIM), bf16),
+            jax.ShapeDtypeStruct((half, HEAD_DIM), bf16),
+            jax.ShapeDtypeStruct((half, 2 * HEAD_DIM), jnp.float32),
+            jax.ShapeDtypeStruct((half, 2 * HEAD_DIM), bf16),
+        ),
+        compiler_params=pltpu.CompilerParams(
+            dimension_semantics=("arbitrary",), vmem_limit_bytes=56 * MIB
+        ),
+        name="attend",
+    )(lists.reshape(-1), counts, core.reshape(1), qg, kv)
+
+    out = jax.ShapeDtypeStruct((rows, width), bf16)
+    return pl.pallas_call(
+        functools.partial(return_kernel, tm_size, hd_size),
+        out_shape=(out, out, out, out),
+        in_specs=[anywhere, anywhere, whole, anywhere],
+        out_specs=(anywhere,) * 4,
+        scratch_shapes=[
+            pltpu.VMEM((half, 2 * HEAD_DIM), bf16),
+            pltpu.VMEM((half, 2 * HEAD_DIM), bf16),
+            dma((4, count)), dma((4, count)), dma((count,)), dma((count,)), dma((4,)),
+        ],
+        compiler_params=pltpu.CompilerParams(
+            collective_id=1, has_side_effects=True, vmem_limit_bytes=60 * MIB
+        ),
+        name="return_tokens",
+    )(o, dq, mine, theirs)
+
+
 def solution(mesh):
     in_specs = (
         P(("tm", "head"), None),
@@ -190,6 +674,7 @@
         P(("tm", "head"), None),
         P(("tm", "head"), None),
     )
+    paired = mesh.shape["tm"] // 2 * mesh.shape["head"] == HEADS
     return jax.shard_map(
-        on_device, mesh=mesh, in_specs=in_specs, out_specs=out_specs, check_vma=False
-    )
+        on_pairs if paired else on_device, mesh=mesh, in_specs=in_specs, out_specs=out_specs, check_vma=False
+    )

time: 924 us -> 262 us (0.28); the launches traced: 908 us -> 261 us
  Pallas kernels: 0 us -> 251 us
  other arithmetic: 235 us -> 0.35 us
  waiting for transfers between devices: 228 us -> 0 us
  local copies, waits for them, and re-layouts: 211 us -> 9.08 us
  matrix products: 133 us -> 0 us
  blocking collectives: 34.4 us -> 0 us
  loops' own time: 30.5 us -> 0 us
  starting transfers between devices: 22.3 us -> 0 us
  between operations: 14.1 us -> 0.71 us
    pallas_call x0 -> x3, Pallas kernels: none -> 251 us  [the longest x1 98.1 us: on_pairs(): pl.pallas_call(functools.partial(return_kernel, tm_size, hd_size), out_sh...]
    dynamic_update_slice x66 -> x0, other arithmetic: 165 us -> none  [add_slabs(): lax.dynamic_update_slice_in_dim(accum, current + parts[slot], where_at, 0)]
    dot_general x12 -> x0, matrix products: 133 us -> none  [the longest x2 28 us: forward_group(): jnp.einsum('tqhd,stkhd->thqsk', grad_tile, values_sel, preferred_element_...]
    while x108 -> x0, local copies, waits for them, and re-layouts: 125 us -> none  [the longest x4 76.8 us: on_device(): sums, outputs = lax.scan(group_with_sums, (zeros, zeros), group_ids)]
    reduce_scatter x2 -> x0, waiting for transfers between devices: 101 us -> none  [the longest x1 83 us: on_device(): lax.psum_scatter(value_fold.reshape(whole_rows, heads_here, HEAD_DIM).ast...]
    all_gather x2 -> x0, waiting for transfers between devices: 88.7 us -> none  [the longest x1 59.4 us: on_device(): lax.all_gather(key_loc, 'tm', axis=0, tiled=True)]
    all_to_all x6 -> x0, waiting for transfers between devices: 37.7 us -> none  [the longest x1 11.6 us: on_device(): lax.all_to_all(grad_out, 'head', split_axis=1, concat_axis=0, tiled=True)]
    all_to_all x2 -> x0, blocking collectives: 34.4 us -> none  [the longest x1 19.1 us: on_device(): lax.all_to_all(value_rows, 'head', split_axis=1, concat_axis=0, tiled=True)]
  transfers between devices with their start and end apart: 10 -> 0, of which waited for: 8 -> 0; matrix products, arithmetic and copies ran while one was open for 10% -> 0% of each run, Pallas kernels for 0% -> 0%
where the time goes in v1:
time: 262 us; the launch traced here: 261 us
  Pallas kernels  251 us (96%)
  local copies, waits for them, and re-layouts  9.08 us (3%)
    pallas_call x1, Pallas kernels, on_pairs(): pl.pallas_call(functools.partial(return_kernel, tm_size, hd_size), out_sh...  98.1 us
    pallas_call x1, Pallas kernels, on_pairs(): pl.pallas_call(functools.partial(scatter_kernel, tm_size, hd_size), out_s...  97.3 us
    pallas_call x1, Pallas kernels, on_pairs(): pl.pallas_call(functools.partial(attend_kernel, tiles_per_shard, slots),...  55.2 us
    unnamed x9, local copies, waits for them, and re-layouts  7.5 us

profile of v1, /device:TPU:0, one launch (start us, length us, event | category | flops | bytes accessed | tf_op | source)
XLA Modules:
  0.0 260.7 jit_solution(8085725110805689122)
XLA Ops:
  0.7 0.8 copy.12
  1.4 0.1 convert_reduce_fusion
  1.6 0.6 reduce_sum.32.counts_ref
  2.2 0.1 copy.13
  2.3 0.1 select_reduce_fusion.1
  2.5 0.1 copy.14
  2.6 0.1 select_reduce_fusion
  2.6 0.1 copy.15
  2.7 0.7 reshape.58.lists_ref
  3.4 97.3 %scatter_heads.1 = (bf16[4096,256]{1,0:T(8,128)(2,1)}, bf16[8192,256]{1,0:T(8,128)(2,1)}) custom-call(bf16[256,2048]{1,0:T(8,128)(2,1)} %q_ref.1, bf16[256,2048]{1,0:T(8,128)(2,1)} %k_ref.1, bf16[256,2048]{1,0:T(8,128)(2,1)} %v_ref.1, bf16[256,2048]{1,0:T(8,128)(2,1)} %g_ref.1), custom_call_target="tpu_custom_call" | custom-call | tf_op jit(solution)/shard_map/scatter_heads/pallas_call | solution.py:579
  100.7 55.2 %attend.1 = (bf16[4096,128]{1,0:T(8,128)(2,1)}, bf16[4096,128]{1,0:T(8,128)(2,1)}, f32[4096,256]{1,0:T(8,128)}, bf16[4096,256]{1,0:T(8,128)(2,1)}) custom-call(s32[544]{0:T(1024)} %reshape.58.lists_ref, s32[32]{0:T(128)} %reduce_sum.32.counts_ref, s32[1]{0:T(128)} %bitcast.2.core_ref, bf16[4096,256]{1,0:T(8,128)(2,1)} %get-tuple-element.10.qg_ref, ...), custom_call_target="tpu_custom_call" | custom-call | tf_op jit(solution)/shard_map/attend/pallas_call | solution.py:610
  155.9 98.1 %return_tokens.1 = (bf16[256,2048]{1,0:T(8,128)(2,1)}, bf16[256,2048]{1,0:T(8,128)(2,1)}, bf16[256,2048]{1,0:T(8,128)(2,1)}, bf16[256,2048]{1,0:T(8,128)(2,1)}) custom-call(bf16[4096,128]{1,0:T(8,128)(2,1)} %get-tuple-element.12.o_ref, bf16[4096,128]{1,0:T(8,128)(2,1)} %get-tuple-element.13.dq_ref, f32[4096,256]{1,0:T(8,128)} %get-tuple-element.14.mine_ref, ...), custom_call_target="tpu_custom_call" | custom-call | tf_op jit(solution)/shard_map/return_tokens/pallas_call | solution.py:646
  254.0 0.0 copy-start.1
  254.0 0.0 copy-start
  254.0 2.5 copy.20
  256.4 2.3 copy.21
  258.7 0.0 copy-done.1
  258.7 1.0 copy.22
  259.7 0.0 copy-done
  259.7 1.0 copy.23
  (3 shorter events, 0.0 us)
Async XLA Ops:
  254.0 4.8 %copy-start.1 = (bf16[256,2048]{1,0:T(8,128)(2,1)S(1)}, bf16[256,2048]{1,0:T(8,128)(2,1)}, u32[]{:S(2)}) copy-start(bf16[256,2048]{1,0:T(8,128)(2,1)} %get-tuple-element.24) | copy-start | bytes 3145732
  254.0 5.7 %copy-start = (bf16[256,2048]{1,0:T(8,128)(2,1)S(1)}, bf16[256,2048]{1,0:T(8,128)(2,1)}, u32[]{:S(2)}) copy-start(bf16[256,2048]{1,0:T(8,128)(2,1)} %get-tuple-element.25) | copy-start | bytes 3145732
